TPU v7x, 256 devices: a whole 4x4x8 slice. The times are simulated.
256 devices in a mesh: dp: 8 (over x, core), mp: 32 (over y, z).
Axes of the slice: x: 4, y: 4, z: 8, core: 2. Of those that a mesh axis runs over, the one named last changes fastest.
Arguments:
- tokens: bfloat16 [4096, 1024], P('dp'), may hold values from -52 to 52
- cotangent: bfloat16 [4096, 1024], P('dp'), may hold values from -12 to 12
- norm_gain: float32 [1024], replicated, may hold values from 0.5 to 1.5
- w_query: bfloat16 [1024, 16384], P(None, 'mp'), may hold values from -0.1875 to 0.1875
- w_key: bfloat16 [1024, 16384], P(None, 'mp'), may hold values from -0.1875 to 0.1875
- w_value: bfloat16 [1024, 16384], P(None, 'mp'), may hold values from -0.1875 to 0.1875
- w_out: bfloat16 [16384, 1024], P('mp'), may hold values from -0.046875 to 0.046875
- bias_table: float32 [128, 32], P('mp'), may hold values from -6 to 252
- buckets: int32 [1023], replicated, may hold values from 0 to 31, as said below
- qkv_rows: float32 [3, 1024], P(None, 'dp'), may hold values from 0.01 to 1
- qkv_cols: float32 [3, 16384], P(None, 'mp'), may hold values from 0.01 to 1
- out_rows: float32 [16384], P('mp'), may hold values from 3 to 300
- out_cols: float32 [1024], P('dp'), may hold values from 3 to 300
Outputs:
- grad_input: float32 [4096, 1024], P('dp')
- norm_gain_grad: float32 [1024], P('dp')
- bias_grad: float32 [128, 32], P('mp', 'dp')
- qkv_update: float32 [3, 1024, 16384], P(None, 'dp', 'mp')
- out_update: float32 [16384, 1024], P('mp', 'dp')
- qkv_rows_new: float32 [3, 1024], P(None, 'dp')
- qkv_cols_new: float32 [3, 16384], P(None, 'mp')
- out_rows_new: float32 [16384], P('mp')
- out_cols_new: float32 [1024], P('dp')
Inputs may be any that keep to these rules, and one draw needn't show every extreme that they name: Entry j - i + 511 is the bucket of key position j seen from query position i of the same sequence. Keys after the query take the upper half of the buckets, the others the lower half; on each side the bucket never falls as the distance grows, distance 0 has bucket 0, and every distance of 128 or more takes that side's last bucket.
All inputs are finite; a program needn't handle non-finite values.
Results may differ from a plain program's by a relative error of at most 0.027.
Values may be sent and summed in bfloat16 or wider, within the bound.
A program may use at most 128 MiB of HBM per device.

v0:
```python
import jax
import jax.numpy as jnp
from jax import lax
from jax.sharding import PartitionSpec as P

D = 1024
DH = 128
NB = 32
LEN = 512
HD = 16384


decay_rate = 1.0 - 100.0 ** (-0.8)


def toeplitz_rows(per_offset, length):
    head_count = per_offset.shape[0]
    padded = jnp.concatenate([per_offset, jnp.zeros((head_count, 1), jnp.float32)], 1)
    repeated = jnp.tile(padded, (1, length))[:, : length * (2 * length - 1)]
    return repeated.reshape(head_count, length, 2 * length - 1)[:, :, length - 1 :]


def diagonal_totals(score_grid, length):
    head_count = score_grid.shape[0]
    widened = jnp.concatenate(
        [jnp.zeros((head_count, length, length - 1), jnp.float32), score_grid], 2
    )
    flattened = widened.reshape(head_count, length * (2 * length - 1))
    flattened = jnp.concatenate([flattened, jnp.zeros((head_count, length), jnp.float32)], 1)
    return jnp.sum(flattened.reshape(head_count, length, 2 * length), 1)[:, : 2 * length - 1]


def norm_backward(d_normed, normal, inverse, norm_gain):
    scaled = d_normed * norm_gain
    centre = jnp.mean(scaled * normal, -1, keepdims=True)
    return ((scaled - normal * centre) * inverse, jnp.sum(d_normed * normal, 0))


def on_device(
    tokens,
    cotangent,
    norm_gain,
    w_query,
    w_key,
    w_value,
    w_out,
    bias_table,
    buckets,
    qkv_rows,
    qkv_cols,
    out_rows,
    out_cols,
):
    scale_factor = DH ** (-0.5)
    token_count = tokens.shape[0]
    seq_count = token_count // LEN
    head_count = bias_table.shape[0]
    local_width = w_query.shape[1]
    float_tokens = tokens.astype(jnp.float32)
    inverse = lax.rsqrt(jnp.mean(float_tokens * float_tokens, -1, keepdims=True) + 1e-06)
    normal = float_tokens * inverse
    normed = (normal * norm_gain).astype(jnp.bfloat16)
    queries = jnp.dot(normed, w_query, preferred_element_type=jnp.float32).astype(jnp.bfloat16)
    key_rows = jnp.dot(normed, w_key, preferred_element_type=jnp.float32).astype(jnp.bfloat16)
    value_rows = jnp.dot(normed, w_value, preferred_element_type=jnp.float32).astype(jnp.bfloat16)

    def split_heads(matrix):
        return matrix.reshape(seq_count, LEN, head_count, DH)

    query_heads = split_heads(queries)
    key_heads = split_heads(key_rows)
    value_heads = split_heads(value_rows)
    onehot = (buckets[:, None] == jnp.arange(NB, dtype=jnp.int32)[None, :]).astype(jnp.float32)
    per_offset = jnp.dot(bias_table, onehot.T, precision=lax.Precision.HIGHEST)
    bias_tile = toeplitz_rows(per_offset, LEN)
    scores = (
        jnp.einsum("sqhd,skhd->shqk", query_heads, key_heads, preferred_element_type=jnp.float32)
        * scale_factor
        + bias_tile[None]
    )
    row_peak = jnp.max(scores, -1, keepdims=True)
    weights = jnp.exp(scores - row_peak)
    attention = weights / jnp.sum(weights, -1, keepdims=True)
    attention_low = attention.astype(jnp.bfloat16)
    attended = (
        jnp.einsum(
            "shqk,skhd->sqhd", attention_low, value_heads, preferred_element_type=jnp.float32
        )
        .astype(jnp.bfloat16)
        .reshape(token_count, local_width)
    )
    d_attended = jnp.einsum(
        "td,ed->te", cotangent, w_out, preferred_element_type=jnp.float32
    ).astype(jnp.bfloat16)
    grad_out_w = jnp.einsum("te,td->ed", attended, cotangent, preferred_element_type=jnp.float32)
    d_att_heads = split_heads(d_attended)
    d_value = (
        jnp.einsum(
            "shqk,sqhd->skhd", attention_low, d_att_heads, preferred_element_type=jnp.float32
        )
        .astype(jnp.bfloat16)
        .reshape(token_count, local_width)
    )
    grad_value = jnp.einsum("td,te->de", normed, d_value, preferred_element_type=jnp.float32)
    value_part = jnp.einsum("te,de->td", d_value, w_value, preferred_element_type=jnp.float32)
    d_probs = jnp.einsum(
        "sqhd,skhd->shqk", d_att_heads, value_heads, preferred_element_type=jnp.float32
    )
    d_scores = attention * (d_probs - jnp.sum(attention * d_probs, -1, keepdims=True))
    d_scores_low = d_scores.astype(jnp.bfloat16)
    d_query = (
        (
            jnp.einsum(
                "shqk,skhd->sqhd", d_scores_low, key_heads, preferred_element_type=jnp.float32
            )
            * scale_factor
        )
        .astype(jnp.bfloat16)
        .reshape(token_count, local_width)
    )
    d_key = (
        (
            jnp.einsum(
                "shqk,sqhd->skhd", d_scores_low, query_heads, preferred_element_type=jnp.float32
            )
            * scale_factor
        )
        .astype(jnp.bfloat16)
        .reshape(token_count, local_width)
    )
    bias_part = jnp.dot(
        diagonal_totals(jnp.sum(d_scores, 0), LEN), onehot, precision=lax.Precision.HIGHEST
    )
    query_key_part = jnp.einsum(
        "te,de->td", d_query, w_query, preferred_element_type=jnp.float32
    ) + jnp.einsum("te,de->td", d_key, w_key, preferred_element_type=jnp.float32)
    grad_query = jnp.einsum("td,te->de", normed, d_query, preferred_element_type=jnp.float32)
    grad_key = jnp.einsum("td,te->de", normed, d_key, preferred_element_type=jnp.float32)
    summed_hidden = lax.psum((value_part + query_key_part).astype(jnp.bfloat16), "mp").astype(
        jnp.float32
    )
    grad_input, gain_part = norm_backward(summed_hidden, normal, inverse, norm_gain)
    grad_query, grad_key, grad_value, grad_outw, gain_grad, bias_grad = (
        lax.psum_scatter(
            grad_query.astype(jnp.bfloat16), "dp", scatter_dimension=0, tiled=True
        ).astype(jnp.float32),
        lax.psum_scatter(
            grad_key.astype(jnp.bfloat16), "dp", scatter_dimension=0, tiled=True
        ).astype(jnp.float32),
        lax.psum_scatter(
            grad_value.astype(jnp.bfloat16), "dp", scatter_dimension=0, tiled=True
        ).astype(jnp.float32),
        lax.psum_scatter(
            grad_out_w.astype(jnp.bfloat16), "dp", scatter_dimension=1, tiled=True
        ).astype(jnp.float32),
        lax.psum_scatter(
            gain_part.astype(jnp.bfloat16), "dp", scatter_dimension=0, tiled=True
        ).astype(jnp.float32),
        lax.psum_scatter(
            bias_part.astype(jnp.bfloat16), "dp", scatter_dimension=1, tiled=True
        ).astype(jnp.float32),
    )
    stacked = jnp.stack([grad_query, grad_key, grad_value])
    stacked_sq = stacked * stacked
    qkv_row_part = jnp.sum(stacked_sq, 2)
    qkv_col_part = jnp.sum(stacked_sq, 1)
    out_sq = grad_outw * grad_outw
    out_row_part = jnp.sum(out_sq, 1)
    out_col_part = jnp.sum(out_sq, 0)
    qkv_row_sum, out_col_sum = lax.psum((qkv_row_part, out_col_part), "mp")
    qkv_col_sum, out_row_sum = lax.psum((qkv_col_part, out_row_part), "dp")
    qkv_rows_new = decay_rate * qkv_rows + (1.0 - decay_rate) * (qkv_row_sum / HD)
    qkv_cols_new = decay_rate * qkv_cols + (1.0 - decay_rate) * (qkv_col_sum / D)
    out_rows_new = decay_rate * out_rows + (1.0 - decay_rate) * (out_row_sum / D)
    out_cols_new = decay_rate * out_cols + (1.0 - decay_rate) * (out_col_sum / HD)
    qkv_raw = stacked * lax.rsqrt(qkv_rows_new[:, :, None] * qkv_cols_new[:, None, :])
    out_raw = grad_outw * lax.rsqrt(out_rows_new[:, None] * out_cols_new[None, :])
    qkv_total, out_total = lax.psum(
        (jnp.sum(qkv_raw * qkv_raw, (1, 2)), jnp.sum(out_raw * out_raw)), ("dp", "mp")
    )
    entry_count = float(D * HD)
    qkv_update = qkv_raw * lax.rsqrt(qkv_total / entry_count + 1e-06)[:, None, None]
    out_update = out_raw * lax.rsqrt(out_total / entry_count + 1e-06)
    return (
        grad_input,
        gain_grad,
        bias_grad,
        qkv_update,
        out_update,
        qkv_rows_new,
        qkv_cols_new,
        out_rows_new,
        out_cols_new,
    )


def solution(mesh):
    return jax.shard_map(
        on_device,
        mesh=mesh,
        in_specs=(
            P("dp", None),
            P("dp", None),
            P(),
            P(None, "mp"),
            P(None, "mp"),
            P(None, "mp"),
            P("mp", None),
            P("mp", None),
            P(),
            P(None, "dp"),
            P(None, "mp"),
            P("mp"),
            P("dp"),
        ),
        out_specs=(
            P("dp", None),
            P("dp"),
            P("mp", "dp"),
            P(None, "dp", "mp"),
            P("mp", "dp"),
            P(None, "dp"),
            P(None, "mp"),
            P("mp"),
            P("dp"),
        ),
        check_vma=False,
    )
```

profile of v0, /device:TPU:1, one launch (start us, length us, event | category | flops | bytes accessed | tf_op | source)
XLA Modules:
  0.0 439.5 jit_solution(16432002320037827113)
XLA Ops:
  8.1 1.6 fusion.8
  9.7 2.2 convolution_convert_fusion.8
  13.3 4.3 broadcast_bitcast_fusion
  17.6 12.0 %copy.63 = f32[1,4,512,1024]{3,1,2,0:T(4,128)} copy(f32[1,4,512,1024]{3,2,1,0:T(8,128)} %broadcast_bitcast_fusion) | data formatting | bytes 16777216
  29.6 7.2 %slice.12 = f32[4,523776]{1,0:T(4,128)} slice(f32[4,524288]{1,0:T(4,128)} %bitcast.69), slice={[0:4], [0:523776]} | slice | bytes 16760832 | tf_op jit(solution)/shard_map/slice | solution.py:19
  36.8 15.7 %reshape.142 = f32[4,512,1023]{2,1,0:T(8,128)} reshape(f32[4,523776]{1,0:T(4,128)} %slice.12) | data formatting | bytes 16760832 | tf_op jit(solution)/shard_map/reshape | solution.py:20
  52.5 5.6 %slice.13 = f32[4,512,512]{2,1,0:T(8,128)} slice(f32[4,512,1023]{2,1,0:T(8,128)} %reshape.142), slice={[0:4], [0:512], [511:1023]} | slice | bytes 8388608 | tf_op jit(solution)/shard_map/slice | solution.py:20
  58.1 5.2 %copy.61 = f32[4,512,512]{1,2,0:T(8,128)} copy(f32[4,512,512]{2,1,0:T(8,128)} %slice.13) | data formatting | bytes 8388608
  63.3 2.9 multiply_add_fusion
  66.3 2.9 fusion.31
  73.4 2.2 fusion.11
  76.1 4.8 %convolution_convert_fusion.5 = bf16[4,128,512]{2,1,0:T(8,128)(2,1)S(1)} fusion(bf16[512,4,128]{0,2,1:T(8,128)(2,1)} %bitcast.94, f32[4,512]{1,0:T(4,128)S(1)} %get-tuple-element.23, f32[4,512,512]{1,2,0:T(8,128)} %copy-done.3), kind=kOutput, calls=%fused_computation.29 | convolution fusion | flops 271845888 | bytes 5251072 | tf_op jit(solution)/shard_map/shqk,sqhd->skhd/dot_general | solution.py:98
  83.2 1.7 add_convert_fusion
  85.0 5.4 %convolution_convert_fusion.4 = bf16[4,128,512]{2,1,0:T(8,128)(2,1)} fusion(bf16[512,4,128]{0,2,1:T(8,128)(2,1)S(1)} %bitcast.92, f32[4,512]{1,0:T(4,128)S(1)} %get-tuple-element.23, f32[4,512,512]{1,2,0:T(8,128)} %copy-done.3), kind=kOutput, calls=%fused_computation.28 | convolution fusion | flops 271845888 | bytes 5251072 | tf_op jit(solution)/shard_map/shqk,skhd->sqhd/dot_general | solution.py:86
  90.4 3.1 convolution_convert_fusion
  93.5 2.3 copy.59
  95.9 1.9 convolution_convert_fusion.2
  97.8 1.9 convolution_convert_fusion.3
  100.2 1.9 convolution_convert_fusion.1
  102.2 5.3 %copy.62 = f32[4,512,512]{2,1,0:T(8,128)} copy(f32[4,512,512]{1,2,0:T(8,128)} %copy-done.2) | data formatting | bytes 8388608
  107.4 7.3 %concatenate.10.clone = f32[4,512,1023]{2,1,0:T(8,128)} pad(f32[4,512,512]{2,1,0:T(8,128)} %copy.62, f32[]{:T(128)} %constant.12.clone.1), padding=0_0x0_0x511_0 | pad | bytes 12574724 | tf_op jit(solution)/shard_map/concatenate | solution.py:25
  114.7 15.1 %reshape.147 = f32[4,523776]{1,0:T(4,128)} reshape(f32[4,512,1023]{2,1,0:T(8,128)} %concatenate.10.clone) | data formatting | bytes 16760832 | tf_op jit(solution)/shard_map/reshape | solution.py:28
  129.8 7.7 %concatenate.11 = f32[4,524288]{1,0:T(4,128)} pad(f32[4,523776]{1,0:T(4,128)} %reshape.147, f32[]{:T(128)} %constant.12.clone.1), padding=0_0x0_512 | pad | bytes 16769028 | tf_op jit(solution)/shard_map/concatenate | solution.py:29
  139.4 7.8 %bitcast_reduce_fusion = f32[4,1024]{1,0:T(4,128)S(1)} fusion(f32[1,4,512,1024]{3,1,2,0:T(4,128)} %bitcast.68), kind=kLoop, calls=%fused_computation.1 | loop fusion | flops 2093056 | bytes 8404992 | tf_op jit(solution)/shard_map/reduce_sum | solution.py:30
  147.6 86.2 %all-reduce.11.cloned.1.call-done = bf16[512,1024]{1,0:T(8,128)(2,1)} async-done(((bf16[512,1024]{1,0:T(8,128)(2,1)}), bf16[512,1024]{1,0:T(8,128)(2,1)}) %all-reduce.11.cloned.1.call-update) | async-done | bytes 1048592 | tf_op jit(solution)/shard_map/psum | solution.py:139
  233.8 2.1 fusion.9
  235.9 17.1 %all-reduce.8 = (bf16[1024]{0:T(1024)(128)(2,1)S(1)}, bf16[4,32]{1,0:T(4,128)(2,1)S(1)}) all-reduce(bf16[1024]{0:T(1024)(128)(2,1)S(1)} %get-tuple-element.9, bf16[4,32]{1,0:T(4,128)(2,1)S(1)} %convolution_convert_fusion.10), channel_id=2, replica_groups=mesh['dp'=8,'mp'=32] {'dp'}, use_global_device_ids=true, to_apply=%region_7.0.clone | all-reduce | flops 1152 | bytes 4608
  253.7 1.8 fusion.5
  258.0 58.3 %all-reduce.6 = (f32[3,128]{1,0:T(4,128)S(1)}, f32[128]{0:T(128)S(1)}) all-reduce(f32[3,128]{1,0:T(4,128)S(1)} %get-tuple-element.11, f32[128]{0:T(128)S(1)} %get-tuple-element.14), channel_id=1, replica_groups=mesh['dp'=8,'mp'=32] {'mp'}, use_global_device_ids=true, to_apply=%region_14.0 | all-reduce | flops 512 | bytes 4096 | tf_op jit(solution)/shard_map/psum | solution.py:170
  316.4 34.9 %all-reduce.7 = (f32[3,512]{1,0:T(4,128)S(1)}, f32[512]{0:T(512)S(1)}) all-reduce(f32[3,512]{1,0:T(4,128)S(1)} %get-tuple-element.12, f32[512]{0:T(512)S(1)} %get-tuple-element.13), channel_id=1, replica_groups=mesh['dp'=8,'mp'=32] {'dp'}, use_global_device_ids=true, to_apply=%region_16.0 | all-reduce | flops 2048 | bytes 16384 | tf_op jit(solution)/shard_map/psum | solution.py:171
  354.0 74.0 %all-reduce.5 = (f32[3]{0:T(128)S(1)}, f32[]{:T(128)}) all-reduce(f32[3]{0:T(128)S(1)} %multiply_reduce_fusion.1, f32[]{:T(128)} %multiply_reduce_fusion.2), channel_id=1, replica_groups=mesh['dp'=8,'mp'=32] {'dp','mp'}, use_global_device_ids=true, to_apply=%region_18.0 | all-reduce | flops 4 | bytes 32 | tf_op jit(solution)/shard_map/psum | solution.py:178
  429.5 2.1 fusion.18
  (97 shorter events, 16.5 us)
Async XLA Ops:
  8.0 1.7 copy-start
  8.0 225.8 %all-reduce.11.cloned.1.call-start = ((), (), s32[]{:S(2)}) async-start(), calls=%async_computation.4 | async-start | bytes 2097152 | tf_op jit(solution)/shard_map/psum | solution.py:139
  9.7 2.3 copy-start.4
  9.7 2.3 copy-start.9
  9.7 2.3 copy-start.14
  12.0 0.9 copy-start.21
  12.0 0.9 copy-start.22
  66.3 2.9 copy-start.3
  66.3 2.9 copy-start.7
  69.3 1.2 copy-start.19
  69.3 1.5 copy-start.20
  70.8 1.5 copy-start.24
  73.4 2.2 copy-start.2
  80.9 1.2 copy-start.8
  81.7 1.2 copy-start.6
  81.7 1.5 copy-start.10
  83.2 1.8 copy-start.25
  84.9 170.6 %reduce-scatter.14.cloned.1.call-start = ((), (), s32[]{:S(2)}) async-start(), calls=%async_computation.8 | async-start | bytes 1179648
  95.8 160.9 %reduce-scatter.10.cloned.1.call-start = ((), (), s32[]{:S(2)}) async-start(), calls=%async_computation.6 | async-start | bytes 1179648 | tf_op jit(solution)/shard_map/reduce_scatter | solution.py:147
  97.8 159.0 %reduce-scatter.8.cloned.1.call-start = ((), (), s32[]{:S(2)}) async-start(), calls=%async_computation.5 | async-start | bytes 1179648 | tf_op jit(solution)/shard_map/reduce_scatter | solution.py:144
  99.8 157.0 %reduce-scatter.12.cloned.1.call-start = ((), (), s32[]{:S(2)}) async-start(), calls=%async_computation.7 | async-start | bytes 1179648 | tf_op jit(solution)/shard_map/reduce_scatter | solution.py:150
  129.8 7.8 %copy-start.27 = (u32[256]{0:T(256)S(1)}, u32[256]{0:T(256)}, u32[]{:S(2)}) copy-start(u32[256]{0:T(256)} %constant.55) | copy-start | bytes 3076
  233.8 19.9 %copy-start.5 = (bf16[512,1024]{1,0:T(8,128)(2,1)S(1)}, bf16[512,1024]{1,0:T(8,128)(2,1)}, u32[]{:S(2)}) copy-start(bf16[512,1024]{1,0:T(8,128)(2,1)} %all-reduce.11.cloned.1.call-done) | copy-start | bytes 3145732
  253.7 62.7 %copy-start.23 = (f32[128]{0:T(128)S(1)}, f32[128]{0:T(128)}, u32[]{:S(2)}) copy-start(f32[128]{0:T(128)} %param.25) | copy-start | bytes 1540
  253.7 97.6 %copy-start.17 = (f32[512]{0:T(512)S(1)}, f32[512]{0:T(512)}, u32[]{:S(2)}) copy-start(f32[512]{0:T(512)} %param.24) | copy-start | bytes 6148
  253.7 98.3 %copy-start.18 = (f32[3,128]{1,0:T(4,128)S(1)}, f32[3,128]{1,0:T(4,128)}, u32[]{:S(2)}) copy-start(f32[3,128]{1,0:T(4,128)} %param.22) | copy-start | bytes 4612
  253.7 98.3 %copy-start.15 = (f32[3,512]{1,0:T(4,128)S(1)}, f32[3,512]{1,0:T(4,128)}, u32[]{:S(2)}) copy-start(f32[3,512]{1,0:T(4,128)} %param.23) | copy-start | bytes 18436
  253.7 178.0 %copy-start.1 = (bf16[1024,512]{1,0:T(8,128)(2,1)S(1)}, bf16[1024,512]{1,0:T(8,128)(2,1)}, u32[]{:S(2)}) copy-start(bf16[1024,512]{1,0:T(8,128)(2,1)} %param.16) | copy-start | bytes 3145732
  316.4 115.3 %copy-start.16 = (f32[128]{0:T(128)}, f32[128]{0:T(128)S(1)}, u32[]{:S(2)}) copy-start(f32[128]{0:T(128)S(1)} %multiply_add_fusion.4) | copy-start | bytes 1540
  351.2 80.4 %copy-start.12 = (f32[512]{0:T(512)}, f32[512]{0:T(512)S(1)}, u32[]{:S(2)}) copy-start(f32[512]{0:T(512)S(1)} %multiply_add_fusion.2) | copy-start | bytes 6148
  352.0 79.7 %copy-start.13 = (f32[3,128]{1,0:T(4,128)}, f32[3,128]{1,0:T(4,128)S(1)}, u32[]{:S(2)}) copy-start(f32[3,128]{1,0:T(4,128)S(1)} %multiply_add_fusion.3) | copy-start | bytes 4612
  352.0 79.6 %copy-start.11 = (f32[3,512]{1,0:T(4,128)}, f32[3,512]{1,0:T(4,128)S(1)}, u32[]{:S(2)}) copy-start(f32[3,512]{1,0:T(4,128)S(1)} %multiply_add_fusion.1) | copy-start | bytes 18436
  (1 other events, 0.8 us)
Sparse Core Ops, SparseCore 0:
  85.0 148.7 all-reduce.10
Sparse Core Ops, SparseCore 1:
  95.9 36.6 reduce-scatter.13
  135.0 33.6 reduce-scatter.9
  171.0 33.4 reduce-scatter.7
  207.1 33.6 reduce-scatter.11
where the time goes:
time: 447 us; the launch traced here: 439 us
  blocking collectives  184 us (41%)
  local copies, waits for them, and re-layouts  90.7 us (20%)
  waiting for transfers between devices  86.3 us (19%)
  matrix products  34.1 us (8%)
  other arithmetic  25 us (6%)
  between operations  18.4 us (4%)
    psum x1, waiting for transfers between devices, on_device(): lax.psum((value_part + query_key_part).astype(jnp.bfloat16), 'mp')  86.2 us
    psum x1, blocking collectives, on_device(): lax.psum((jnp.sum(qkv_raw * qkv_raw, (1, 2)), jnp.sum(out_raw * out_raw))...  74 us
    psum x1, blocking collectives, on_device(): qkv_row_sum, out_col_sum = lax.psum((qkv_row_part, out_col_part), 'mp')  58.3 us
    psum x1, blocking collectives, on_device(): qkv_col_sum, out_row_sum = lax.psum((qkv_col_part, out_row_part), 'dp')  34.9 us
    unnamed x63, local copies, waits for them, and re-layouts  32.1 us
    unnamed x1, blocking collectives  17.1 us
    reshape x1, local copies, waits for them, and re-layouts, toeplitz_rows(): repeated.reshape(head_count, length, 2 * length - 1)[:, :, length - 1:]  15.7 us
    reshape x1, local copies, waits for them, and re-layouts, diagonal_totals(): flattened = widened.reshape(head_count, length * (2 * length - 1))  15.1 us
  transfers between devices with their start and end apart: 5, of which 1 were waited for; matrix products, arithmetic and copies ran while one was open for 15% of the time, Pallas kernels for 0%

commit v1 on v0

v1 whole, which is shorter than its diff:
```python
import functools

import jax
import jax.numpy as jnp
from jax import lax
from jax.experimental import pallas as pl
from jax.experimental.pallas import tpu as pltpu
from jax.sharding import PartitionSpec as P

D = 1024
DH = 128
NB = 32
LEN = 512
HD = 16384
HEADS = 4
N_DP = 8
N_Y = 4
N_Z = 8
SCALE = DH ** (-0.5)
DECAY = 1.0 - 100.0 ** (-0.8)
MESH = pl.DeviceIdType.MESH
BF = jnp.bfloat16
F32 = jnp.float32


def nn(a, b):
    return lax.dot_general(a, b, (((1,), (0,)), ((), ())), preferred_element_type=F32)


def nt(a, b):
    return lax.dot_general(a, b, (((1,), (1,)), ((), ())), preferred_element_type=F32)


def exact(a, b, contract):
    return lax.dot_general(
        a,
        b,
        ((contract[:1], contract[1:]), ((), ())),
        preferred_element_type=F32,
        precision=lax.Precision.HIGHEST,
    )


def kernel(
    tokens,
    cot,
    gain,
    w_query,
    w_key,
    w_value,
    w_out,
    table,
    reversed_buckets,
    qkv_rows,
    qkv_cols,
    out_rows,
    out_cols,
    grad_input,
    gain_grad,
    bias_grad,
    qkv_update,
    out_update,
    qkv_rows_new,
    qkv_cols_new,
    out_rows_new,
    out_cols_new,
    normed,
    normed_t,
    cot_t,
    normal,
    q_heads,
    k_heads,
    v_heads,
    da_heads,
    bias_rows,
    diagonals,
    att_low,
    ds_low,
    dq_all,
    dk_all,
    dv_all,
    onehot,
    grads,
    core_in,
    ring_a,
    ring_b,
    ring_l,
    ring_r,
    total,
    hidden,
    y_a,
    y_b,
    y_l,
    y_r,
    z_out,
    z_in,
    gathered,
    dp_box,
    y_box,
    z_box,
    last_box,
    core_send,
    core_recv,
    x_send,
    x_recv,
    y_send,
    y_recv,
    zs_send,
    zs_recv,
    zg_send,
    zg_recv,
    yg_send,
    yg_recv,
    dp_send,
    dp_recv,
    yb_send,
    yb_recv,
    zb_send,
    zb_recv,
    last_send,
    last_recv,
):
    dp = lax.axis_index("dp")
    mp = lax.axis_index("mp")
    core = lax.rem(dp, 2)
    x = lax.div(dp, 2)
    y = lax.div(mp, N_Z)
    z = lax.rem(mp, N_Z)

    def at_x(k):
        return lax.rem(x + k, 4)

    def at_y(k):
        return lax.rem(y + k, 4)

    def at_z(k):
        return lax.rem(z + k, N_Z)

    def dp_peer(k):
        return {"dp": lax.rem(dp + k, N_DP)}

    def x_peer(k):
        return {"dp": at_x(k) * 2 + core}

    def y_peer(k):
        return {"mp": at_y(k) * N_Z + z}

    def z_peer(k):
        return {"mp": y * N_Z + at_z(k)}

    barrier = pltpu.get_barrier_semaphore()
    for k in range(1, N_DP):
        pl.semaphore_signal(barrier, inc=1, device_id=dp_peer(k), device_id_type=MESH)
    for k in range(1, 4):
        pl.semaphore_signal(barrier, inc=1, device_id=y_peer(k), device_id_type=MESH)
    for k in range(1, N_Z):
        pl.semaphore_signal(barrier, inc=1, device_id=z_peer(k), device_id_type=MESH)

    def remote(src, dst, send, recv, peer):
        return pltpu.make_async_remote_copy(
            src_ref=src, dst_ref=dst, send_sem=send, recv_sem=recv, device_id=peer, device_id_type=MESH
        )

    floats = tokens[...].astype(F32)
    inverse = lax.rsqrt(jnp.mean(floats * floats, -1, keepdims=True) + 1e-06)
    normal[...] = floats * inverse
    normed[...] = (normal[...] * gain[...]).astype(BF)
    normed_t[...] = normed[...].T
    cot_t[...] = cot[...].T
    onehot[...] = (
        reversed_buckets[...] == lax.broadcasted_iota(jnp.int32, (NB, 1024), 0)
    ).astype(F32)
    per_offset = exact(table[...], onehot[...], (1, 0))
    for h in range(HEADS):
        wide = jnp.broadcast_to(per_offset[h : h + 1, :], (128, 1024))
        bias_rows[h] = pltpu.roll(wide, 897, 1, stride=1, stride_axis=0)
    for matrix, heads in ((w_query, q_heads), (w_key, k_heads), (w_value, v_heads)):
        product = nn(normed[...], matrix[...]).astype(BF)
        for h in range(HEADS):
            heads[h] = product[:, h * DH : (h + 1) * DH]
    product = nt(cot[...], w_out[...]).astype(BF)
    for h in range(HEADS):
        da_heads[h] = product[:, h * DH : (h + 1) * DH]

    def attend(h):
        query, key, value, d_att = q_heads[h], k_heads[h], v_heads[h], da_heads[h]
        started = set()
        for i in range(4):
            cols = slice(i * 128, (i + 1) * 128)
            scores = nt(key, query[cols, :]) * SCALE
            scores = scores + jnp.concatenate(
                [bias_rows[h, :, (i - b + 3) * 128 : (i - b + 4) * 128] for b in range(4)], 0
            )
            weights = jnp.exp(scores - jnp.max(scores, 0, keepdims=True))
            attention = weights * (1.0 / jnp.sum(weights, 0, keepdims=True))
            att_low[:, cols] = attention.astype(BF)
            d_probs = nt(value, d_att[cols, :])
            d_scores = attention * (d_probs - jnp.sum(attention * d_probs, 0, keepdims=True))
            ds_low[:, cols] = d_scores.astype(BF)
            for b in range(4):
                t = i - b + 3
                lanes = slice(t * 128, (t + 1) * 128)
                tile = d_scores[b * 128 : (b + 1) * 128, :]
                if t in started:
                    diagonals[h, :, lanes] = diagonals[h, :, lanes] + tile
                else:
                    diagonals[h, :, lanes] = tile
                    started.add(t)
        diagonals[h, :, 896:1024] = jnp.zeros((128, 128), F32)
        d_value = nn(att_low[...], d_att).astype(BF)
        d_key = (nn(ds_low[...], query) * SCALE).astype(BF)
        attended = nn(value.T, att_low[...]).astype(BF).T
        d_query = (nn(key.T, ds_low[...]) * SCALE).astype(BF).T
        lanes = pl.ds(pl.multiple_of(h * DH, DH), DH)
        dq_all[:, lanes] = d_query
        dk_all[:, lanes] = d_key
        dv_all[:, lanes] = d_value
        return attended, jnp.concatenate([d_query, d_key, d_value], 1)

    def weight_grads(h, attended, joined):
        for r in range(2):
            block = nn(normed_t[r * 512 : (r + 1) * 512, :], joined).astype(BF)
            last = nn(cot_t[r * 512 : (r + 1) * 512, :], attended).astype(BF)
            for s in range(4):
                p = r * 4 + s
                rows = slice(s * 128, (s + 1) * 128)
                for m in range(3):
                    grads[h, p % 2, p // 2, m * 128 : (m + 1) * 128, :] = block[
                        rows, m * 128 : (m + 1) * 128
                    ]
                grads[h, p % 2, p // 2, 384:512, :] = last[rows, :]

    top, low = slice(0, 256), slice(256, 512)

    def core_copy(h):
        return remote(
            grads.at[h, 1 - core], core_in.at[h], core_send.at[h], core_recv.at[h], {"dp": x * 2 + 1 - core}
        )

    def x_copy(h, n):
        src, dst, peer = (
            (grads.at[h, core, at_x(2), top], ring_a.at[h], 1),
            (grads.at[h, core, at_x(2), low], ring_b.at[h], 3),
            (grads.at[h, core, at_x(1), low], ring_r.at[h, low], 1),
            (grads.at[h, core, at_x(3), top], ring_l.at[h, top], 3),
            (grads.at[h, core, at_x(1), top], ring_r.at[h, top], 1),
            (grads.at[h, core, at_x(3), low], ring_l.at[h, low], 3),
        )[n]
        return remote(src, dst, x_send.at[h, n], x_recv.at[h, n], x_peer(peer))

    def add_into(ref, index, other):
        ref[index] = (ref[index].astype(F32) + other.astype(F32)).astype(BF)

    def x_first(h):
        core_copy(h).wait_recv()
        for k in (2, 1, 3, 0):
            add_into(grads, (h, core, at_x(k)), core_in[h, at_x(k)])
            if k == 2:
                x_copy(h, 0).start()
                x_copy(h, 1).start()
            elif k == 1:
                x_copy(h, 2).start()
            elif k == 3:
                x_copy(h, 3).start()

    def x_second(h):
        x_copy(h, 0).wait_recv()
        add_into(grads, (h, core, at_x(1), top), ring_a[h])
        x_copy(h, 4).start()
        x_copy(h, 1).wait_recv()
        add_into(grads, (h, core, at_x(3), low), ring_b[h])
        x_copy(h, 5).start()

    def x_third(h):
        for n in range(2, 6):
            x_copy(h, n).wait_recv()
        whole = grads[h, core, x].astype(F32) + ring_r[h].astype(F32) + ring_l[h].astype(F32)
        lanes = pl.ds(pl.multiple_of(h * DH, DH), DH)
        for m in range(4):
            total[m, :, lanes] = whole[m * 128 : (m + 1) * 128, :]

    pl.semaphore_wait(barrier, (N_DP - 1) + 3 + (N_Z - 1))

    def per_head(h, carry):
        attended, joined = attend(h)

        @pl.when(h >= 1)
        def _():
            x_first(h - 1)

        weight_grads(h, attended, joined)
        core_copy(h).start()

        @pl.when(h >= 1)
        def _():
            x_second(h - 1)

        @pl.when(h >= 2)
        def _():
            x_third(h - 2)

        return carry

    lax.fori_loop(0, HEADS, per_head, 0)

    gain_parts = []
    for c in range(4):
        cols = slice(c * 256, (c + 1) * 256)
        piece = (
            nt(dq_all[...], w_query[cols, :])
            + nt(dk_all[...], w_key[cols, :])
            + nt(dv_all[...], w_value[cols, :])
        )
        gain_parts.append(jnp.sum(piece * normal[:, cols], 0, keepdims=True))
        hidden[:, :, cols] = piece.astype(BF).reshape(4, 128, 256)

    y_top, y_low = slice(0, 64), slice(64, 128)

    def y_copy(n):
        src, dst, peer = (
            (hidden.at[at_y(2), y_top], y_a, 1),
            (hidden.at[at_y(2), y_low], y_b, 3),
            (hidden.at[at_y(1), y_low], y_r.at[y_low], 1),
            (hidden.at[at_y(3), y_top], y_l.at[y_top], 3),
            (hidden.at[at_y(1), y_top], y_r.at[y_top], 1),
            (hidden.at[at_y(3), y_low], y_l.at[y_low], 3),
        )[n]
        return remote(src, dst, y_send.at[n], y_recv.at[n], y_peer(peer))

    for n in range(4):
        y_copy(n).start()
    x_first(HEADS - 1)
    x_third(HEADS - 2)

    folded = diagonals[...]
    rows = 64
    while rows >= 8:
        folded = folded[:, :rows, :] + pltpu.roll(
            folded[:, rows:, :].reshape(HEADS * rows, 1024), 1024 - rows, 1
        ).reshape(HEADS, rows, 1024)
        rows //= 2
    sums = []
    for h in range(HEADS):
        line = folded[h, 0:1, :]
        for r in range(1, 8):
            line = line + pltpu.roll(folded[h, r : r + 1, :], 1024 - r, 1)
        sums.append(pltpu.roll(line, 127, 1))
    bias_part = exact(jnp.concatenate(sums, 0), onehot[...], (1, 1))

    y_copy(0).wait_recv()
    add_into(hidden, (at_y(1), y_top), y_a[...])
    y_copy(4).start()
    y_copy(1).wait_recv()
    add_into(hidden, (at_y(3), y_low), y_b[...])
    y_copy(5).start()
    x_second(HEADS - 1)

    def zs_copy(k):
        return remote(z_out.at[at_z(k)], z_in.at[k - 1], zs_send.at[k - 1], zs_recv.at[k - 1], z_peer(k))

    for n in range(2, 6):
        y_copy(n).wait_recv()
    z_out[...] = (
        (hidden[y].astype(F32) + y_r[...].astype(F32) + y_l[...].astype(F32))
        .astype(BF)
        .reshape(N_Z, 16, D)
    )
    for k in (4, 3, 5, 2, 6, 1, 7):
        zs_copy(k).start()

    x_third(HEADS - 1)
    dp_box[dp, 0:4, :] = jnp.concatenate(
        [jnp.sum(total[m] * total[m], 0, keepdims=True) for m in range(4)], 0
    )
    dp_box[dp, 4:5, :] = jnp.concatenate(gain_parts[:2], 1)
    dp_box[dp, 5:6, :] = jnp.concatenate(gain_parts[2:], 1)
    dp_box[dp, 6:8, :] = jnp.zeros((2, 512), F32)
    dp_box[dp, 8:16, :] = jnp.zeros((8, 512), F32)
    dp_box[dp, 8:12, 0:NB] = bias_part

    def dp_copy(k):
        return remote(dp_box.at[dp], dp_box.at[dp], dp_send.at[k - 1], dp_recv.at[k - 1], dp_peer(k))

    def dp_arrival(k):
        source = lax.rem(dp + N_DP - k, N_DP)
        return remote(dp_box.at[source], dp_box.at[source], dp_send.at[k - 1], dp_recv.at[k - 1], dp_peer(k))

    for k in range(1, N_DP):
        dp_copy(k).start()

    for k in range(1, N_Z):
        zs_copy(k).wait_recv()
    d_normed = z_out[z].astype(F32)
    for k in range(1, N_Z):
        d_normed = d_normed + z_in[k - 1].astype(F32)
    own = pl.ds(pl.multiple_of(mp * 16, 16), 16)
    own_floats = tokens[own, :].astype(F32)
    own_inverse = lax.rsqrt(jnp.mean(own_floats * own_floats, -1, keepdims=True) + 1e-06)
    own_normal = own_floats * own_inverse
    scaled = d_normed * gain[...]
    centre = jnp.mean(scaled * own_normal, -1, keepdims=True)
    gathered[y, z] = ((scaled - own_normal * centre) * own_inverse).astype(BF)

    def zg_copy(k):
        return remote(gathered.at[y, z], gathered.at[y, z], zg_send.at[k - 1], zg_recv.at[k - 1], z_peer(k))

    def zg_arrival(k):
        source = at_z(N_Z - k)
        return remote(gathered.at[y, source], gathered.at[y, source], zg_send.at[k - 1], zg_recv.at[k - 1], z_peer(k))

    for k in (4, 3, 5, 2, 6, 1, 7):
        zg_copy(k).start()

    for k in range(1, N_DP):
        dp_arrival(k).wait_recv()
    summed = dp_box[0]
    for s in range(1, N_DP):
        summed = summed + dp_box[s]
    bias_grad[...] = summed[8:12, 0:128]
    cols_old = jnp.concatenate([qkv_cols[...], out_rows[...]], 0)
    cols_new = DECAY * cols_old + (1.0 - DECAY) * (summed[0:4, :] / D)
    qkv_cols_new[...] = cols_new[0:3, :]
    out_rows_new[...] = cols_new[3:4, :]
    half = pl.ds(pl.multiple_of(lax.rem(dp, 4) * 128, 128), 128)
    line = lax.div(dp, 4)
    own_gain = jnp.zeros((1, 128), F32)
    for s in range(N_DP):
        pair = dp_box[s, 4:6, half]
        own_gain = own_gain + jnp.where(line == 0, pair[0:1, :], pair[1:2, :])
    lane = lax.broadcasted_iota(jnp.int32, (128, 128), 1)
    packed = jnp.zeros((128, 128), F32)
    for m in range(4):
        squared = total[m] * total[m]
        packed = jnp.where(lane == m, jnp.sum(squared, 1, keepdims=True), packed)
        weighted = jnp.sum(squared / cols_new[m : m + 1, :], 1, keepdims=True)
        packed = jnp.where(lane == m + 4, weighted, packed)
    y_box[y, 0:8, :] = packed.T[0:8, :]
    y_box[y, 8:16, :] = jnp.broadcast_to(own_gain, (8, 128))

    def yb_copy(k):
        return remote(y_box.at[y], y_box.at[y], yb_send.at[k - 1], yb_recv.at[k - 1], y_peer(k))

    def yb_arrival(k):
        source = at_y(4 - k)
        return remote(y_box.at[source], y_box.at[source], yb_send.at[k - 1], yb_recv.at[k - 1], y_peer(k))

    for k in range(1, 4):
        yb_copy(k).start()

    def yg_copy(n):
        first, second = pl.ds(0, 4), pl.ds(4, 4)
        ref, peer = (
            (gathered.at[y], 1),
            (gathered.at[y], 3),
            (gathered.at[at_y(3), first], 1),
            (gathered.at[at_y(1), second], 3),
        )[n]
        return remote(ref, ref, yg_send.at[n], yg_recv.at[n], y_peer(peer))

    def yg_arrival(n):
        first, second = pl.ds(0, 4), pl.ds(4, 4)
        ref = (
            gathered.at[at_y(3)],
            gathered.at[at_y(1)],
            gathered.at[at_y(2), first],
            gathered.at[at_y(2), second],
        )[n]
        return remote(ref, ref, yg_send.at[n], yg_recv.at[n], y_peer(1))

    for k in range(1, N_Z):
        zg_arrival(k).wait_recv()
    yg_copy(0).start()
    yg_copy(1).start()

    for k in range(1, 4):
        yb_arrival(k).wait_recv()
    z_box[z] = y_box[0] + y_box[1] + y_box[2] + y_box[3]

    def zb_copy(k):
        return remote(z_box.at[z], z_box.at[z], zb_send.at[k - 1], zb_recv.at[k - 1], z_peer(k))

    def zb_arrival(k):
        source = at_z(N_Z - k)
        return remote(z_box.at[source], z_box.at[source], zb_send.at[k - 1], zb_recv.at[k - 1], z_peer(k))

    for k in range(1, N_Z):
        zb_copy(k).start()

    yg_arrival(0).wait_recv()
    yg_copy(2).start()
    yg_arrival(1).wait_recv()
    yg_copy(3).start()

    for k in range(1, N_Z):
        zb_arrival(k).wait_recv()
    row_sums = z_box[0]
    for s in range(1, N_Z):
        row_sums = row_sums + z_box[s]
    gain_grad[...] = row_sums[8:9, :]
    rows_old = jnp.concatenate([qkv_rows[...], out_cols[...]], 0)
    rows_new = DECAY * rows_old + (1.0 - DECAY) * (row_sums[0:4, :] / HD)
    qkv_rows_new[...] = rows_new[0:3, :]
    out_cols_new[...] = rows_new[3:4, :]
    ratio = row_sums[4:8, :] / rows_new
    last_box[dp] = jnp.concatenate([ratio, jnp.zeros((4, 128), F32)], 0)

    def last_copy(k):
        return remote(last_box.at[dp], last_box.at[dp], last_send.at[k - 1], last_recv.at[k - 1], dp_peer(k))

    def last_arrival(k):
        source = lax.rem(dp + N_DP - k, N_DP)
        return remote(last_box.at[source], last_box.at[source], last_send.at[k - 1], last_recv.at[k - 1], dp_peer(k))

    for k in range(1, N_DP):
        last_copy(k).start()

    for n in range(2, 4):
        yg_arrival(n).wait_recv()
    grad_input[...] = gathered[...].astype(F32).reshape(LEN, D)

    for k in range(1, N_DP):
        last_arrival(k).wait_recv()
    raw_total = last_box[0]
    for s in range(1, N_DP):
        raw_total = raw_total + last_box[s]
    mean_square = jnp.sum(raw_total, 1, keepdims=True) / float(D * HD)
    row_scale = jnp.concatenate(
        [lax.rsqrt(rows_new) * lax.rsqrt(mean_square[0:4, :] + 1e-06), jnp.zeros((124, 128), F32)], 0
    ).T
    for m in range(4):
        update = total[m] * row_scale[:, m : m + 1] * lax.rsqrt(cols_new[m : m + 1, :])
        if m < 3:
            qkv_update[m] = update
        else:
            out_update[...] = update.T

    def drain(h, carry):
        core_copy(h).wait_send()
        for n in range(6):
            x_copy(h, n).wait_send()
        return carry

    lax.fori_loop(0, HEADS, drain, 0)
    for n in range(6):
        y_copy(n).wait_send()
    for k in range(1, N_Z):
        zs_copy(k).wait_send()
        zg_copy(k).wait_send()
        zb_copy(k).wait_send()
    for n in range(4):
        yg_copy(n).wait_send()
    for k in range(1, 4):
        yb_copy(k).wait_send()
    for k in range(1, N_DP):
        dp_copy(k).wait_send()
        last_copy(k).wait_send()


def pairs(*shape):
    return [pltpu.SemaphoreType.DMA(shape)] * 2


def on_device(
    tokens,
    cotangent,
    norm_gain,
    w_query,
    w_key,
    w_value,
    w_out,
    bias_table,
    buckets,
    qkv_rows,
    qkv_cols,
    out_rows,
    out_cols,
):
    reversed_buckets = jnp.concatenate([buckets[::-1], jnp.full((1,), -1, jnp.int32)])[None]
    vmem = pl.BlockSpec(memory_space=pltpu.VMEM)
    outs = pl.pallas_call(
        kernel,
        out_shape=[
            jax.ShapeDtypeStruct((LEN, D), F32),
            jax.ShapeDtypeStruct((1, 128), F32),
            jax.ShapeDtypeStruct((HEADS, 128), F32),
            jax.ShapeDtypeStruct((3, 128, 512), F32),
            jax.ShapeDtypeStruct((512, 128), F32),
            jax.ShapeDtypeStruct((3, 128), F32),
            jax.ShapeDtypeStruct((3, 512), F32),
            jax.ShapeDtypeStruct((1, 512), F32),
            jax.ShapeDtypeStruct((1, 128), F32),
        ],
        in_specs=[vmem] * 13,
        out_specs=[vmem] * 9,
        scratch_shapes=[
            pltpu.VMEM((LEN, D), BF),
            pltpu.VMEM((D, LEN), BF),
            pltpu.VMEM((D, LEN), BF),
            pltpu.VMEM((LEN, D), F32),
            pltpu.VMEM((HEADS, LEN, DH), BF),
            pltpu.VMEM((HEADS, LEN, DH), BF),
            pltpu.VMEM((HEADS, LEN, DH), BF),
            pltpu.VMEM((HEADS, LEN, DH), BF),
            pltpu.VMEM((HEADS, 128, 1024), F32),
            pltpu.VMEM((HEADS, 128, 1024), F32),
            pltpu.VMEM((LEN, LEN), BF),
            pltpu.VMEM((LEN, LEN), BF),
            pltpu.VMEM((LEN, HEADS * DH), BF),
            pltpu.VMEM((LEN, HEADS * DH), BF),
            pltpu.VMEM((LEN, HEADS * DH), BF),
            pltpu.VMEM((NB, 1024), F32),
            pltpu.VMEM((HEADS, 2, 4, 512, DH), BF),
            pltpu.VMEM((HEADS, 4, 512, DH), BF),
            pltpu.VMEM((HEADS, 256, DH), BF),
            pltpu.VMEM((HEADS, 256, DH), BF),
            pltpu.VMEM((HEADS, 512, DH), BF),
            pltpu.VMEM((HEADS, 512, DH), BF),
            pltpu.VMEM((4, 128, 512), F32),
            pltpu.VMEM((4, 128, D), BF),
            pltpu.VMEM((64, D), BF),
            pltpu.VMEM((64, D), BF),
            pltpu.VMEM((128, D), BF),
            pltpu.VMEM((128, D), BF),
            pltpu.VMEM((N_Z, 16, D), BF),
            pltpu.VMEM((N_Z - 1, 16, D), BF),
            pltpu.VMEM((4, N_Z, 16, D), BF),
            pltpu.VMEM((N_DP, 16, 512), F32),
            pltpu.VMEM((4, 16, 128), F32),
            pltpu.VMEM((N_Z, 16, 128), F32),
            pltpu.VMEM((N_DP, 8, 128), F32),
            *pairs(HEADS),
            *pairs(HEADS, 6),
            *pairs(6),
            *pairs(N_Z - 1),
            *pairs(N_Z - 1),
            *pairs(4),
            *pairs(N_DP - 1),
            *pairs(3),
            *pairs(N_Z - 1),
            *pairs(N_DP - 1),
        ],
        compiler_params=pltpu.CompilerParams(
            collective_id=0, has_side_effects=True, vmem_limit_bytes=56 * 1024 * 1024
        ),
    )(
        tokens,
        cotangent,
        norm_gain[None],
        w_query,
        w_key,
        w_value,
        w_out,
        bias_table,
        reversed_buckets,
        qkv_rows,
        qkv_cols,
        out_rows[None],
        out_cols[None],
    )
    grad_input, gain, bias, qkv_update, out_update, rows_new, cols_new, orows_new, ocols_new = outs
    bias = lax.dynamic_slice_in_dim(bias[:, :NB], lax.axis_index("dp") * 4, 4, 1)
    return (
        grad_input,
        gain[0],
        bias,
        qkv_update,
        out_update,
        rows_new,
        cols_new,
        orows_new[0],
        ocols_new[0],
    )


def solution(mesh):
    return jax.shard_map(
        on_device,
        mesh=mesh,
        in_specs=(
            P("dp", None),
            P("dp", None),
            P(),
            P(None, "mp"),
            P(None, "mp"),
            P(None, "mp"),
            P("mp", None),
            P("mp", None),
            P(),
            P(None, "dp"),
            P(None, "mp"),
            P("mp"),
            P("dp"),
        ),
        out_specs=(
            P("dp", None),
            P("dp"),
            P("mp", "dp"),
            P(None, "dp", "mp"),
            P("mp", "dp"),
            P(None, "dp"),
            P(None, "mp"),
            P("mp"),
            P("dp"),
        ),
        check_vma=False,
    )
```

time: 447 us -> 85.8 us (0.19); the launches traced: 439 us -> 85.7 us
  blocking collectives: 184 us -> 0 us
  waiting for transfers between devices: 86.3 us -> 0 us
  local copies, waits for them, and re-layouts: 90.7 us -> 9.75 us
  Pallas kernels: 0 us -> 74.6 us
  matrix products: 34.1 us -> 0 us
  other arithmetic: 25 us -> 0.67 us
  between operations: 18.4 us -> 0.68 us
    psum x3 -> x0, blocking collectives: 167 us -> none  [the longest x1 74 us: on_device(): lax.psum((jnp.sum(qkv_raw * qkv_raw, (1, 2)), jnp.sum(out_raw * out_raw))...]
    psum x1 -> x0, waiting for transfers between devices: 86.2 us -> none  [on_device(): lax.psum((value_part + query_key_part).astype(jnp.bfloat16), 'mp')]
    pallas_call x0 -> x1, Pallas kernels: none -> 74.6 us  [on_device(): pl.pallas_call(kernel, out_shape=[jax.ShapeDtypeStruct((LEN, D), F32), ja...]
    dot_general x19 -> x0, matrix products: 34.1 us -> none  [the longest x1 5.44 us: on_device(): jnp.einsum('shqk,skhd->sqhd', attention_low, value_heads, preferred_eleme...]
    reshape x2 -> x0, local copies, waits for them, and re-layouts: 30.7 us -> none  [the longest x1 15.7 us: toeplitz_rows(): repeated.reshape(head_count, length, 2 * length - 1)[:, :, length - 1:]]
    unnamed x63 -> x24, local copies, waits for them, and re-layouts: 32.1 us -> 8.47 us
    unnamed x1 -> x0, blocking collectives: 17.1 us -> none
    concatenate x3 -> x0, local copies, waits for them, and re-layouts: 15.1 us -> none  [the longest x1 7.75 us: diagonal_totals(): jnp.concatenate([flattened, jnp.zeros((head_count, length), jnp.float32)]...]
  transfers between devices with their start and end apart: 5 -> 0, of which waited for: 1 -> 0; matrix products, arithmetic and copies ran while one was open for 15% -> 0% of each run, Pallas kernels for 0% -> 0%
where the time goes in v1:
time: 85.8 us; the launch traced here: 85.7 us
  Pallas kernels  74.6 us (87%)
  local copies, waits for them, and re-layouts  9.75 us (11%)
    pallas_call x1, Pallas kernels, on_device(): pl.pallas_call(kernel, out_shape=[jax.ShapeDtypeStruct((LEN, D), F32), ja...  74.6 us
    unnamed x24, local copies, waits for them, and re-layouts  8.47 us

profile of v1, /device:TPU:1, one launch (start us, length us, event | category | flops | bytes accessed | tf_op | source)
XLA Modules:
  0.0 85.7 jit_solution(400415323607409815)
XLA Ops:
  0.6 0.8 reverse
  1.4 0.1 slice.4
  1.5 0.7 pad_add_fusion
  2.1 74.6 %shard_map.196 = (f32[512,1024]{1,0:T(8,128)}, f32[1,128]{1,0:T(1,128)}, f32[4,128]{1,0:T(4,128)}, f32[3,128,512]{2,1,0:T(8,128)}, f32[512,128]{1,0:T(8,128)}, /...) custom-call(bf16[512,1024]{1,0:T(8,128)(2,1)} %tokens.1, bf16[512,1024]{1,0:T(8,128)(2,1)} %cot.1, ...), custom_call_target="tpu_custom_call" | custom-call | tf_op jit(solution)/shard_map/pallas_call | solution.py:580
  76.7 1.3 %constant_dynamic-slice_fusion = f32[4,4]{1,0:T(4,128)} fusion(f32[4,32]{1,0:T(4,128)} %bitcast.14, s32[]{:T(128)S(6)} %select_n.3), kind=kLoop, calls=%fused_computation.1 | loop fusion | bytes 132 | tf_op jit(solution)/shard_map/dynamic_slice | solution.py:661
  78.0 0.0 copy-start.6
  78.0 0.0 copy-start
  78.0 0.0 copy-start.1
  78.0 3.2 %copy.30 = f32[512,1024]{1,0:T(8,128)} copy(f32[512,1024]{1,0:T(8,128)} %get-tuple-element.36) | data formatting | bytes 4194304
  81.3 0.0 copy-done.6
  81.3 0.0 copy-start.4
  81.3 0.0 copy-start.2
  81.3 0.0 copy-start.3
  81.3 0.0 copy-start.5
  81.3 0.5 copy.31
  81.8 0.0 copy-done
  81.8 0.9 %copy.32 = f32[3,128,512]{2,1,0:T(8,128)} copy(f32[3,128,512]{2,1,0:T(8,128)S(1)} %copy-done) | data formatting | bytes 1572864
  82.7 0.0 copy-done.1
  82.7 0.7 copy.33
  83.4 0.0 copy-done.4
  83.4 0.6 copy.34
  84.0 0.0 copy-done.2
  84.0 0.6 copy.35
  84.6 0.0 copy-done.3
  84.6 0.6 copy.36
  85.2 0.0 copy-done.5
  85.2 0.5 copy.37
Async XLA Ops:
  78.0 3.3 %copy-start.6 = (f32[1,128]{1,0:T(1,128)S(1)}, f32[1,128]{1,0:T(1,128)}, u32[]{:S(2)}) copy-start(f32[1,128]{1,0:T(1,128)} %get-tuple-element.19) | copy-start | bytes 1540
  78.0 3.8 %copy-start = (f32[3,128,512]{2,1,0:T(8,128)S(1)}, f32[3,128,512]{2,1,0:T(8,128)}, u32[]{:S(2)}) copy-start(f32[3,128,512]{2,1,0:T(8,128)} %get-tuple-element.39) | copy-start | bytes 2359300
  78.0 4.7 %copy-start.1 = (f32[512,128]{1,0:T(8,128)S(1)}, f32[512,128]{1,0:T(8,128)}, u32[]{:S(2)}) copy-start(f32[512,128]{1,0:T(8,128)} %get-tuple-element.40) | copy-start | bytes 786436
  81.3 2.1 %copy-start.4 = (f32[3,128]{1,0:T(4,128)S(1)}, f32[3,128]{1,0:T(4,128)}, u32[]{:S(2)}) copy-start(f32[3,128]{1,0:T(4,128)} %get-tuple-element.41) | copy-start | bytes 4612
  81.3 2.7 %copy-start.2 = (f32[3,512]{1,0:T(4,128)S(1)}, f32[3,512]{1,0:T(4,128)}, u32[]{:S(2)}) copy-start(f32[3,512]{1,0:T(4,128)} %get-tuple-element.42) | copy-start | bytes 18436
  81.3 3.3 %copy-start.3 = (f32[1,512]{1,0:T(1,128)S(1)}, f32[1,512]{1,0:T(1,128)}, u32[]{:S(2)}) copy-start(f32[1,512]{1,0:T(1,128)} %get-tuple-element.25) | copy-start | bytes 6148
  81.3 3.9 %copy-start.5 = (f32[1,128]{1,0:T(1,128)S(1)}, f32[1,128]{1,0:T(1,128)}, u32[]{:S(2)}) copy-start(f32[1,128]{1,0:T(1,128)} %get-tuple-element.26) | copy-start | bytes 1540
